TPU v7x, 256 devices: a whole 4x4x8 slice. The times are simulated.
256 devices in a mesh: bricks: 64 (over y, z, core), slab: 4 (over x).
Axes of the slice: x: 4, y: 4, z: 8, core: 2. Of those that a mesh axis runs over, the one named last changes fastest.
Arguments:
- part_pos: float32 [256, 3, 2048], P(('bricks', 'slab')), may hold values from 0 to 1, as said below
- part_mass: float32 [256, 2048], P(('bricks', 'slab')), may hold values from 0.5 to 2
- cell_pos: float32 [256, 3, 2048], P(('bricks', 'slab')), may hold values from 0 to 1, as said below
- cell_mass: float32 [256, 2048], P(('bricks', 'slab')), may hold values from 0.5 to 2
- cell_scale: float32 [256, 2048], P(('bricks', 'slab')), may hold values from 0.5 to 2
- req_tile: int32 [16384, 1], P(('bricks', 'slab')), may hold values from 0 to 15, as said below
- tile_bucket: int32 [256, 144], P(('bricks', 'slab')), may hold values from 0 to 15, as said below
- tile_slot: int32 [256, 144], P(('bricks', 'slab')), may hold values from 0 to 63, as said below
- tile_count: int32 [256], P(('bricks', 'slab')), may hold values from 64 to 144, as said below
- lagr_index: int32 [256, 2048], P(('bricks', 'slab')), may hold values from 0 to 2047, each once within a row
Outputs:
- particle_potential: float32 [256, 2048], P(('bricks', 'slab'))
- cell_potential: float32 [256, 2048], P(('bricks', 'slab'))
- divergence: float32 [16, 256, 128], P('slab', 'bricks')
Inputs may be any that keep to these rules, and one draw needn't show every extreme that they name: `part_pos`: device b * 4 + s holds particles of its own brick: component 0 within [0.25 b / 64, 0.25 (b + 1) / 64], component 1 within [0.25 s / 4, 0.25 (s + 1) / 4], component 2 within [0, 1]. `cell_pos`: device b * 4 + s holds the cells of the same brick, bounded as its particles. `req_tile`: over the devices of one slab index, every cell tile of every device is named by exactly four slots. `tile_bucket`: A device's live tiles name each of its buckets at least once. `tile_slot`: A device's live tiles name each of its slots at least once. `tile_count`: the live tiles are the first entries of a device's list; one device has exactly 144, every other between 64 and 80. `lagr_index`: each device's particles fill its block of the Lagrangian grid, one point each.
All inputs are finite; a program needn't handle non-finite values.
Results may differ from a plain program's by a relative error of at most 0.0003.
Values sent between devices are 32-bit elements; how exact they have to be, the bound alone decides.
A program may use at most 64 MiB of HBM per device.

v0:
```python
import jax
import jax.numpy as jnp
from jax import lax
from jax.sharding import PartitionSpec as P

TS = 128
ITERS = 2
LB = 4


EPS = 0.05
tile_group = 16


def with_halo(block, sides, width):
    for axis, dim in sides:
        count = lax.axis_size(axis)
        forward = [(i, i + 1) for i in range(count - 1)]
        backward = [(target, source) for source, target in forward]
        low = lax.ppermute(
            lax.slice_in_dim(block, block.shape[dim] - width, None, axis=dim), axis, forward
        )
        high = lax.ppermute(lax.slice_in_dim(block, 0, width, axis=dim), axis, backward)
        block = jnp.concatenate([low, block, high], axis=dim)
    return block


def tile_kernel(part_tiles, cell_tiles, live_mask):
    distance = (part_tiles[:, 0, :, None] - cell_tiles[:, 0, None, :]) ** 2
    distance = distance + (part_tiles[:, 1, :, None] - cell_tiles[:, 1, None, :]) ** 2
    distance = distance + (part_tiles[:, 2, :, None] - cell_tiles[:, 2, None, :]) ** 2
    return jnp.exp(-distance / EPS) * live_mask[:, None, None]


def grouped(arrays):
    return tuple(
        (
            item.reshape((item.shape[0] // tile_group, tile_group) + item.shape[1:])
            for item in arrays
        )
    )


def row_pass(part_rows, cell_rows, live_mask, buckets, value_rows, bucket_count):

    def row_one_group(pieces):
        part_piece, cell_piece, mask_piece, value_piece = pieces
        kernel = tile_kernel(part_piece, cell_piece, mask_piece)
        return jnp.einsum("tij,tcj->tci", kernel, value_piece, precision=lax.Precision.HIGHEST)

    per_tile = lax.map(row_one_group, grouped((part_rows, cell_rows, live_mask, value_rows)))
    per_tile = per_tile.reshape((-1,) + per_tile.shape[2:])
    one_hot = (buckets[:, None] == jnp.arange(bucket_count, dtype=jnp.int32)[None, :]).astype(
        jnp.float32
    )
    return jnp.einsum("tb,tci->bci", one_hot, per_tile, precision=lax.Precision.HIGHEST)


def column_pass(part_rows, cell_rows, live_mask, slot_ids, scale_rows, slot_total):

    def column_one_group(pieces):
        part_piece, cell_piece, mask_piece, scale_piece = pieces
        kernel = tile_kernel(part_piece, cell_piece, mask_piece)
        return jnp.einsum("tij,ti->tj", kernel, scale_piece, precision=lax.Precision.HIGHEST)

    per_tile = lax.map(column_one_group, grouped((part_rows, cell_rows, live_mask, scale_rows)))
    per_tile = per_tile.reshape((-1,) + per_tile.shape[2:])
    one_hot = (slot_ids[:, None] == jnp.arange(slot_total, dtype=jnp.int32)[None, :]).astype(
        jnp.float32
    )
    return jnp.einsum("ts,tj->sj", one_hot, per_tile, precision=lax.Precision.HIGHEST)


def on_device(
    part_pos,
    part_mass,
    cell_pos,
    cell_mass,
    cell_scale,
    req_tile,
    tile_bucket,
    tile_slot,
    tile_count,
    lagr_index,
):
    places = part_pos[0]
    tile_width = TS
    bucket_count = places.shape[1] // tile_width
    cell_tiles = cell_pos.shape[2] // tile_width
    brick_count = lax.axis_size("bricks")
    per_peer = req_tile.shape[1]
    slot_total = brick_count * per_peer
    part_tiles = places.reshape(3, bucket_count, tile_width).transpose(1, 0, 2)
    own_cells = cell_pos[0].reshape(3, cell_tiles, tile_width).transpose(1, 0, 2)
    buckets = tile_bucket[0]
    slot_ids = tile_slot[0]
    live_mask = (jnp.arange(buckets.shape[0], dtype=jnp.int32) < tile_count[0]).astype(jnp.float32)
    cell_ids = jnp.arange(cell_tiles, dtype=jnp.int32)
    wanted = (jnp.arange(brick_count, dtype=jnp.int32)[:, None] * cell_tiles + req_tile).reshape(
        slot_total
    )
    every_cell = lax.all_gather(own_cells, "bricks", axis=0, tiled=True)
    slot_cells = every_cell[wanted]

    def fetch_duals(values):
        return lax.all_gather(values, "bricks", axis=0, tiled=True)[wanted]

    part_rows = part_tiles[buckets]
    cell_rows = slot_cells[slot_ids]
    masses = part_mass[0].reshape(bucket_count, tile_width)
    cell_masses = cell_mass[0].reshape(cell_tiles, tile_width)
    cell_scaling = cell_scale[0].reshape(cell_tiles, tile_width)
    for sweep in range(ITERS):
        fetched = fetch_duals(cell_scaling[:, None, :])
        totals = row_pass(part_rows, cell_rows, live_mask, buckets, fetched[slot_ids], bucket_count)
        particle_scale = masses / totals[:, 0]
        partial_value = column_pass(
            part_rows, cell_rows, live_mask, slot_ids, particle_scale[buckets], slot_total
        )
        one_hot = (req_tile[:, :, None] == cell_ids[None, None, :]).astype(jnp.float32)
        dense_sums = jnp.einsum(
            "pcq,pct->pqt",
            one_hot,
            partial_value.reshape(brick_count, per_peer, tile_width),
            precision=lax.Precision.HIGHEST,
        )
        cell_scaling = cell_masses / lax.psum_scatter(
            dense_sums.reshape(brick_count * cell_tiles, tile_width),
            "bricks",
            scatter_dimension=0,
            tiled=True,
        )
    weighted = jnp.concatenate(
        [cell_scaling[:, None, :], cell_scaling[:, None, :] * own_cells], axis=1
    )
    fetched = fetch_duals(weighted)
    totals = row_pass(part_rows, cell_rows, live_mask, buckets, fetched[slot_ids], bucket_count)
    particle_scale = masses / totals[:, 0]
    displacement = totals[:, 1:] / totals[:, 0:1] - part_tiles
    displacement = displacement.transpose(1, 0, 2).reshape(3, bucket_count * tile_width)
    lagr_grid = jnp.zeros_like(displacement).at[:, lagr_index[0]].set(displacement)
    planes = lagr_grid.reshape(3, -1, LB, tile_width)
    across = with_halo(planes[0], (("slab", 0),), 1)
    second = with_halo(planes[1], (("bricks", 1),), 1)
    depth_pad = jnp.pad(planes[2], ((0, 0), (0, 0), (1, 1)))
    divergence = 0.5 * (across[2:] - across[:-2])
    divergence = divergence + 0.5 * (second[:, 2:] - second[:, :-2])
    divergence = divergence + 0.5 * (depth_pad[:, :, 2:] - depth_pad[:, :, :-2])
    particle_potential = jnp.log(particle_scale).reshape(1, -1)
    cell_potential = jnp.log(cell_scaling).reshape(1, -1)
    return (particle_potential, cell_potential, divergence)


def solution(mesh):
    return jax.shard_map(
        on_device,
        mesh=mesh,
        in_specs=(
            P(("bricks", "slab"), None, None),
            P(("bricks", "slab"), None),
            P(("bricks", "slab"), None, None),
            P(("bricks", "slab"), None),
            P(("bricks", "slab"), None),
            P(("bricks", "slab"), None),
            P(("bricks", "slab"), None),
            P(("bricks", "slab"), None),
            P(("bricks", "slab")),
            P(("bricks", "slab"), None),
        ),
        out_specs=(
            P(("bricks", "slab"), None),
            P(("bricks", "slab"), None),
            P("slab", "bricks", None),
        ),
        check_vma=False,
    )
```

profile of v0, /device:TPU:1, one launch (start us, length us, event | category | flops | bytes accessed | tf_op | source)
XLA Modules:
  0.0 640.3 jit_solution(7654722147235039259)
XLA Ops:
  11.5 54.9 %all_gather.13 = f32[1024,1,128]{2,0,1:T(8,128)S(1)} all-gather(f32[16,1,128]{2,0,1:T(8,128)} %bitcast.349), channel_id=1, replica_groups=mesh['bricks'=64,'slab'=4] {'bricks'}, dimensions={0}, use_global_device_ids=true | all-gather | bytes 532480 | tf_op jit(solution)/shard_map/all_gather | solution.py:106
  68.5 18.0 %all-gather.4.cloned.1.call-done = f32[1024,3,128]{2,0,1:T(8,128)} async-done(((f32[16,3,128]{2,0,1:T(8,128)}), f32[1024,3,128]{2,0,1:T(8,128)}) %all-gather.4.cloned.1.call-update) | async-done | bytes 1572880 | tf_op jit(solution)/shard_map/all_gather | solution.py:102
  90.6 24.3 %while.50 = (s32[]{:T(128)}, f32[9,16,1,128]{3,2,1,0:T(1,128)S(1)}, f32[9,16,1,128]{3,2,1,0:T(1,128)S(1)}, f32[9,16,3,128]{3,2,1,0:T(4,128)S(1)}, f32[9,16,3,128...) while((s32[]{:T(128)}, f32[9,16,1,128]{3,2,1,0:T(1,128)S(1)}, f32[9,16,1,128]{3,2,1,0:T(1,128)S(1)}, ...), condition=%wide.region_1.2_spmd, body=%wide.region_0.1_spmd.sunk | while | flops 6029314 | bytes 263893 | solution.py:51
  90.7 2.6 fusion.197
  93.4 2.6 fusion.197
  96.1 2.6 fusion.197
  98.8 2.6 fusion.197
  101.5 2.6 fusion.197
  104.2 2.6 fusion.197
  106.9 2.6 fusion.197
  109.6 2.6 fusion.197
  112.3 2.6 fusion.197
  115.8 18.7 %while.51 = (s32[]{:T(128)}, f32[9,16,128]{2,1,0:T(8,128)S(1)}, f32[9,16,3,128]{3,2,1,0:T(4,128)S(1)}, f32[9,16,3,128]{3,2,1,0:T(4,128)S(1)}, f32[9,16]{1,0:T(8,128)S(1)}, /*index=5*/f32[9,16,128]{2,1,0:T(8,128)S(1)}, s32[]{:T(128)}) while((s32[]{:T(128)}, f32[9,16,128]{2,1,0:T(8,128)S(1)}, f32[9,16,3,128]{3,2,1,0:T(4,128)S(1)}, ...), condition=%wide.region_3.4_spmd, body=%wide.region_2.3_spmd.sunk | while | flops 6029314 | bytes 295197 | solution.py:66
  135.9 132.3 %reduce-scatter.3.cloned.1.call-done = f32[16,128]{1,0:T(8,128)} async-done(((f32[1024,128]{1,0:T(8,128)}), f32[16,128]{1,0:T(8,128)}) %reduce-scatter.3.cloned.1.call-update) | async-done | bytes 8208 | tf_op jit(solution)/shard_map/reduce_scatter | solution.py:127
  268.9 54.8 %all-gather = f32[1024,128]{1,0:T(8,128)S(1)} all-gather(f32[16,128]{1,0:T(8,128)S(1)} %div.42), channel_id=2, replica_groups=mesh['bricks'=64,'slab'=4] {'bricks'}, dimensions={0}, use_global_device_ids=true | all-gather | bytes 532480 | tf_op jit(solution)/shard_map/all_gather | solution.py:106
  325.0 24.3 %while.52 = (s32[]{:T(128)}, f32[9,16,1,128]{3,2,1,0:T(1,128)S(1)}, f32[9,16,1,128]{3,2,1,0:T(1,128)S(1)}, f32[9,16,3,128]{3,2,1,0:T(4,128)S(1)}, f32[9,16,3,128...) while((s32[]{:T(128)}, f32[9,16,1,128]{3,2,1,0:T(1,128)S(1)}, f32[9,16,1,128]{3,2,1,0:T(1,128)S(1)}, ...), condition=%wide.region_6.7_spmd, body=%wide.region_5.6_spmd.sunk | while | flops 6029314 | bytes 263893 | solution.py:51
  325.2 2.6 fusion.209
  327.9 2.6 fusion.209
  330.6 2.6 fusion.209
  333.3 2.6 fusion.209
  336.0 2.6 fusion.209
  338.7 2.6 fusion.209
  341.4 2.6 fusion.209
  350.2 18.7 %while.53 = (s32[]{:T(128)}, f32[9,16,128]{2,1,0:T(8,128)S(1)}, f32[9,16,3,128]{3,2,1,0:T(4,128)S(1)}, f32[9,16,3,128]{3,2,1,0:T(4,128)S(1)}, f32[9,16]{1,0:T(8,128)S(1)}, /*index=5*/f32[9,16,128]{2,1,0:T(8,128)S(1)}, s32[]{:T(128)}) while((s32[]{:T(128)}, f32[9,16,128]{2,1,0:T(8,128)S(1)}, f32[9,16,3,128]{3,2,1,0:T(4,128)S(1)}, ...), condition=%wide.region_8.9_spmd, body=%wide.region_7.8_spmd.sunk | while | flops 6029314 | bytes 295197 | solution.py:66
  370.4 132.0 %reduce-scatter.5.cloned.1.call-done = f32[16,128]{1,0:T(8,128)} async-done(((f32[1024,128]{1,0:T(8,128)}), f32[16,128]{1,0:T(8,128)}) %reduce-scatter.5.cloned.1.call-update) | async-done | bytes 8208 | tf_op jit(solution)/shard_map/reduce_scatter | solution.py:127
  504.4 81.7 %all-gather.6.cloned.1.call-done = f32[1024,4,128]{2,1,0:T(4,128)} async-done(((f32[16,4,128]{2,1,0:T(4,128)}), f32[1024,4,128]{2,1,0:T(4,128)}) %all-gather.6.cloned.1.call-update) | async-done | bytes 2097168 | tf_op jit(solution)/shard_map/all_gather | solution.py:106
  589.2 24.2 %while.54 = (s32[]{:T(128)}, f32[9,16,4,128]{3,2,1,0:T(4,128)S(1)}, f32[9,16,4,128]{3,2,1,0:T(4,128)S(1)}, f32[9,16,3,128]{3,1,2,0:T(8,128)S(1)}, f32[9,16,3,128...) while((s32[]{:T(128)}, f32[9,16,4,128]{3,2,1,0:T(4,128)S(1)}, f32[9,16,4,128]{3,2,1,0:T(4,128)S(1)}, ...), condition=%wide.region_11.12_spmd, body=%wide.region_10.11_spmd.sunk | while | flops 15466498 | bytes 313049 | solution.py:51
  597.3 2.6 fusion.219
  610.7 2.6 fusion.219
  613.9 5.8 scatter_custom_fusion
  623.6 3.4 collective-permute-start.3
  628.4 4.0 collective-permute-start.1
  (323 shorter events, 90.0 us)
Async XLA Ops:
  7.2 61.2 %copy-start.7 = (s32[64,1]{0,1:T(1,128)S(1)}, s32[64,1]{0,1:T(1,128)}, u32[]{:S(2)}) copy-start(s32[64,1]{0,1:T(1,128)} %param.25) | copy-start | bytes 772
  7.2 79.3 %all-gather.4.cloned.1.call-start = ((), (), s32[]{:S(2)}) async-start(), calls=%async_computation.2 | async-start | bytes 1597440 | tf_op jit(solution)/shard_map/all_gather | solution.py:102
  7.9 260.3 %reduce-scatter.3.cloned.1.call-start = ((), (), s32[]{:S(2)}) async-start(), calls=%async_computation.3 | async-start | bytes 532480 | tf_op jit(solution)/shard_map/reduce_scatter | solution.py:127
  90.6 24.3 %copy-start.2 = (f32[1,2048]{1,0:T(1,128)S(1)}, f32[1,2048]{1,0:T(1,128)}, u32[]{:S(2)}) copy-start(f32[1,2048]{1,0:T(1,128)} %param.21) | copy-start | bytes 24580
  90.6 24.3 %copy-start.4 = (s32[1,144]{1,0:T(1,128)S(1)}, s32[1,144]{1,0:T(1,128)}, u32[]{:S(2)}) copy-start(s32[1,144]{1,0:T(1,128)} %param.26) | copy-start | bytes 1732
  115.8 18.7 %copy-start.5 = (s32[1,144]{1,0:T(1,128)S(1)}, s32[1,144]{1,0:T(1,128)}, u32[]{:S(2)}) copy-start(s32[1,144]{1,0:T(1,128)} %param.27) | copy-start | bytes 1732
  115.8 152.4 %copy-start.3 = (f32[1,2048]{1,0:T(1,128)S(1)}, f32[1,2048]{1,0:T(1,128)}, u32[]{:S(2)}) copy-start(f32[1,2048]{1,0:T(1,128)} %param.23) | copy-start | bytes 24580
  135.9 366.5 %reduce-scatter.5.cloned.1.call-start = ((), (), s32[]{:S(2)}) async-start(), calls=%async_computation.4 | async-start | bytes 532480 | tf_op jit(solution)/shard_map/reduce_scatter | solution.py:127
  350.2 153.4 %copy-start = (f32[1,3,2048]{2,0,1:T(1,128)S(1)}, f32[1,3,2048]{2,0,1:T(1,128)}, u32[]{:S(2)}) copy-start(f32[1,3,2048]{2,0,1:T(1,128)} %param.22) | copy-start | bytes 73732
  350.2 154.1 %copy-start.6 = (s32[1,2048]{1,0:T(1,128)S(1)}, s32[1,2048]{1,0:T(1,128)}, u32[]{:S(2)}) copy-start(s32[1,2048]{1,0:T(1,128)} %param.29) | copy-start | bytes 24580
  370.3 215.8 %all-gather.6.cloned.1.call-start = ((), (), s32[]{:S(2)}) async-start(), calls=%async_computation.5 | async-start | bytes 2129920 | tf_op jit(solution)/shard_map/all_gather | solution.py:106
  589.1 24.4 %copy-start.1 = (f32[1,3,2048]{2,0,1:T(1,128)S(1)}, f32[1,3,2048]{2,0,1:T(1,128)}, u32[]{:S(2)}) copy-start(f32[1,3,2048]{2,0,1:T(1,128)} %param.20) | copy-start | bytes 73732
  621.5 11.5 %collective-permute-start.2 = (f32[4,1,128]{2,1,0:T(1,128)S(1)}, f32[4,1,128]{2,1,0:T(1,128)S(1)}, u32[]{:S(2)}, u32[]{:S(2)}) collective-permute-start(f32[4,1,128]{2,1,0:T(1,128)S(1)} %get-tuple-element.398), channel_id=1, source_target_pairs={{4,0},{8,4},{12,8},{16,12},{20,16},{24,20},{28,24},{32,28},{36,32}... | collective-permute-start | bytes 6152 | tf_op jit(solution)/shard_map/ppermute | solution.py:23
  623.6 9.4 %collective-permute-start.3 = (f32[4,1,128]{2,1,0:T(1,128)S(1)}, f32[4,1,128]{2,1,0:T(1,128)S(1)}, u32[]{:S(2)}, u32[]{:S(2)}) collective-permute-start(f32[4,1,128]{2,1,0:T(1,128)S(1)} %get-tuple-element.399), channel_id=1, source_target_pairs={{0,4},{4,8},{8,12},{12,16},{16,20},{20,24},{24,28},{28,32},{32,36}... | collective-permute-start | bytes 6152 | tf_op jit(solution)/shard_map/ppermute | solution.py:20
  627.1 5.9 collective-permute-start
  628.4 4.7 collective-permute-start.1
Sparse Core Ops, SparseCore 0:
  10.6 75.8 all-gather.3
  136.0 132.1 reduce-scatter.2
  370.4 131.8 reduce-scatter.4
  505.0 81.0 all-gather.5
where the time goes:
time: 642 us; the launch traced here: 640 us
  waiting for transfers between devices  365 us (57%)
  blocking collectives  110 us (17%)
  matrix products  106 us (17%)
  local copies, waits for them, and re-layouts  24.4 us (4%)
  between operations  14.7 us (2%)
  starting transfers between devices  11 us (2%)
  other arithmetic  7.51 us (1%)
    reduce_scatter x2, waiting for transfers between devices, on_device(): lax.psum_scatter(dense_sums.reshape(brick_count * cell_tiles, tile_width)...  264 us
    all_gather x2, blocking collectives, fetch_duals(): return lax.all_gather(values, 'bricks', axis=0, tiled=True)[wanted]  110 us
    all_gather x1, waiting for transfers between devices, fetch_duals(): return lax.all_gather(values, 'bricks', axis=0, tiled=True)[wanted]  81.7 us
    dot_general x27, matrix products, row_one_group(): jnp.einsum('tij,tcj->tci', kernel, value_piece, precision=lax.Precision.H...  70 us
    dot_general x18, matrix products, column_one_group(): jnp.einsum('tij,ti->tj', kernel, scale_piece, precision=lax.Precision.HIG...  35 us
    all_gather x1, waiting for transfers between devices, on_device(): every_cell = lax.all_gather(own_cells, 'bricks', axis=0, tiled=True)  18 us
  transfers between devices with their start and end apart: 8, of which 5 were waited for; matrix products, arithmetic and copies ran while one was open for 1% of the time, Pallas kernels for 0%

commit v1 on v0

v1 whole, which is shorter than its diff:
```python
import functools
import math

import jax
import jax.numpy as jnp
from jax import lax
from jax.experimental import pallas as pl
from jax.experimental.pallas import tpu as pltpu
from jax.sharding import PartitionSpec as P

TS = 128
EPS = 0.05
ITERS = 2
LB = 4
SCALE = math.sqrt(2.0 / (EPS * math.log(2.0)))
CENTER = (0.125, 0.125, 0.5)
HALF_LN2 = 0.5 * math.log(2.0)
MESH = pl.DeviceIdType.MESH
F32, BF16, I32 = jnp.float32, jnp.bfloat16, jnp.int32
TL = 256


def split3(a):
    hi = a.astype(BF16)
    rest = a - hi.astype(F32)
    mid = rest.astype(BF16)
    return hi, mid, (rest - mid.astype(F32)).astype(BF16)


def pick(hot, rows):
    hi, mid, lo = split3(rows)
    return jnp.dot(
        jnp.concatenate([hot, hot, hot], axis=1),
        jnp.concatenate([hi, mid, lo], axis=0),
        preferred_element_type=F32,
    )


def iota(shape, axis):
    return lax.broadcasted_iota(I32, shape, axis)


def kernel(
    nb, ns, buckets, tiles, count,
    pos_in, mass_in, cpos_in, cmass_in, cscale_in, req_in, tb_in, ts_in, cnt_in, lagr_in,
    pp_out, cp_out, div_out,
    ask, asked, lists_v, lists, xs, ys, rowsets, xb, mb, ub, kt, seg, colseg,
    pay, cells, wsend, wrecv, vsend, vrecv, vy, hot_l, field, halo,
    ssem, rsem, hsem, lsem,
):
    me, sl = lax.axis_index("bricks"), lax.axis_index("slab")
    up, down = lax.rem(me + 1, nb), lax.rem(me + nb - 1, nb)
    right, left = lax.rem(sl + 1, ns), lax.rem(sl + ns - 1, ns)

    barrier = pltpu.get_barrier_semaphore()

    def greet(k, carry):
        pl.semaphore_signal(
            barrier, inc=1, device_id=(lax.rem(me + k, nb), sl), device_id_type=MESH
        )
        return carry

    lax.fori_loop(1, nb, greet, 0)
    for other in (left, right):
        pl.semaphore_signal(barrier, inc=1, device_id=(me, other), device_id_type=MESH)

    def send_all(src, dst, phase):
        def one(k, carry):
            peer = lax.rem(me + k, nb)
            pltpu.make_async_remote_copy(
                src_ref=src.at[peer], dst_ref=dst.at[me],
                send_sem=ssem.at[phase], recv_sem=rsem.at[phase],
                device_id=(peer, sl), device_id_type=MESH,
            ).start()
            return carry

        lax.fori_loop(1, nb, one, 0)
        pltpu.make_async_copy(src.at[me], dst.at[me], rsem.at[phase]).start()

    def wait_all(dst, phase):
        pltpu.make_async_copy(dst, dst, rsem.at[phase]).wait()

    def wait_sent(src, phase):
        part = src.at[pl.ds(0, nb - 1)]
        pltpu.make_async_copy(part, part, ssem.at[phase]).wait()

    ask[...] = jnp.broadcast_to(req_in[...], ask.shape)

    pl.semaphore_wait(barrier, nb + 1)
    send_all(ask, asked, 0)

    lane = iota((1, TL), 1)
    live = lane < cnt_in[0]
    tb = jnp.concatenate([tb_in[...], jnp.zeros((1, TL - count), I32)], axis=1)
    ts = jnp.concatenate([ts_in[...], jnp.zeros((1, TL - count), I32)], axis=1)
    key_b = jnp.where(live, tb, buckets)
    key_s = jnp.where(live, ts, nb)
    uni_b, uni_s = key_b * TL + lane, key_s * TL + lane
    zero = jnp.zeros((1, TL), I32)
    cols = jnp.concatenate([uni_b, uni_s, tb, ts, key_b, key_s, zero, zero], axis=0).T
    col_tb, col_ts, col_kb, col_ks = (cols[:, i : i + 1] for i in range(2, 6))

    def total(where, value):
        return jnp.sum(jnp.where(where, value, 0), axis=0, keepdims=True)

    rank_b = total(cols[:, 0:1] < uni_b, 1)
    rank_s = total(cols[:, 1:2] < uni_s, 1)
    ranks = jnp.concatenate([rank_b, rank_s] + [zero] * 6, axis=0).T
    wide = iota((TL, TL), 1)
    at_b, at_s = ranks[:, 0:1] == wide, ranks[:, 1:2] == wide

    def same(row):
        return jnp.where((row == pltpu.roll(row, 1, 1)) & (lane > 0), 1, 0)

    def within(row, most):
        return jnp.minimum(jnp.maximum(row, 0), most)

    lists_v[0:1, :] = within(total(at_b, col_tb), buckets - 1)
    lists_v[1:2, :] = within(total(at_b, col_ts), nb - 1)
    lists_v[2:3, :] = same(total(at_b, col_kb))
    lists_v[3:4, :] = within(total(at_s, ranks[:, 0:1]), count - 1)
    lists_v[4:5, :] = within(total(at_s, col_tb), buckets - 1)
    lists_v[5:6, :] = same(total(at_s, col_ks))
    lists_v[6:7, :] = within(total(col_kb <= wide, 1) - 1, count - 1)
    lists_v[7:8, :] = within(total(col_ks <= wide, 1) - 1, count - 1)
    to_smem = pltpu.make_async_copy(lists_v, lists, lsem)
    to_smem.start()

    for q in range(buckets):
        part = pl.ds(q * TS, TS)
        rowsets[0, q : q + 1, :] = mass_in[:, part]
        for m in range(3):
            xs[m, q : q + 1, :] = (pos_in[0, m : m + 1, part] - CENTER[m]) * SCALE
    for q in range(tiles):
        part = pl.ds(q * TS, TS)
        rowsets[1, q : q + 1, :] = cmass_in[:, part]
        rowsets[2, q : q + 1, :] = cscale_in[:, part]
        for m in range(3):
            ys[m, q : q + 1, :] = (cpos_in[0, m : m + 1, part] - CENTER[m]) * SCALE
    ysq = ys[0] * ys[0] + ys[1] * ys[1] + ys[2] * ys[2]
    scaled = rowsets[2] * jnp.exp2(-0.5 * ysq)
    offer = jnp.concatenate([ys[0], ys[1], ys[2], scaled, rowsets[1]], axis=1)

    columns = jnp.concatenate([xs[0], xs[1], xs[2], rowsets[0]], axis=0).T
    for q in range(buckets):
        for m in range(3):
            xb[m, q] = jnp.broadcast_to(columns[:, m * buckets + q : m * buckets + q + 1], (TS, TS))
        mb[q] = jnp.broadcast_to(columns[:, 3 * buckets + q : 3 * buckets + q + 1], (TS, TS))

    wait_all(asked, 0)
    asks = asked[...].astype(F32)
    hot = jnp.where(asks[:, 0:tiles] == iota((nb, tiles), 1).astype(F32), 1.0, 0.0).astype(BF16)
    chosen = pick(hot, offer)
    for m in range(4):
        pay[:, m, :] = chosen[:, m * TS : (m + 1) * TS]
    send_all(pay, cells, 1)
    cmass_of = chosen[:, 4 * TS :]
    asks_t = asks.T
    twins = jnp.where(asks[:, 0:nb] == asks_t[0:nb, :], 1.0, 0.0).astype(BF16)
    hot_t = jnp.where(asks_t[0:tiles, :] == iota((tiles, nb), 0).astype(F32), 1.0, 0.0).astype(BF16)

    for q in range(buckets):
        vy[0, q : q + 1, :] = lagr_in[:, pl.ds(q * TS, TS)].astype(F32)
    spots = vy[0, 0:buckets, :]
    spots_c = jnp.concatenate([spots, jnp.zeros((TS - buckets, TS), F32)], axis=0).T
    for q in range(buckets):
        spot = jnp.broadcast_to(spots_c[:, q : q + 1], (TS, TS)).astype(I32)
        hot_l[q] = jnp.where(lax.rem(spot, TS) == iota((TS, TS), 1), 1.0, 0.0).astype(BF16)

    to_smem.wait()
    wait_all(cells, 1)

    def build(k, total):
        b, s = lists[0, k], lists[1, k]
        exponent = xb[0, b] * cells[s, 0:1] + xb[1, b] * cells[s, 1:2] + xb[2, b] * cells[s, 2:3]
        tile = jnp.exp2(exponent)
        kt[k] = tile
        total = jnp.where(lists[2, k] > 0, total, 0.0) + tile * cells[s, 3:4]
        seg[k] = total
        return total

    lax.fori_loop(0, count, build, jnp.zeros((TS, TS), F32), unroll=4)

    def row_pass(value):
        def step(k, total):
            total = jnp.where(lists[2, k] > 0, total, 0.0) + kt[k] * value(lists[1, k])
            seg[k] = total
            return total

        lax.fori_loop(0, count, step, jnp.zeros((TS, TS), F32), unroll=4)

    def col_pass(phase):
        def scale(q, carry):
            ub[q] = mb[q] / jnp.sum(seg[lists[6, q]], axis=1, keepdims=True)
            return carry

        lax.fori_loop(0, buckets, scale, 0, unroll=2)

        def step(k, total):
            product = kt[lists[3, k]] * ub[lists[4, k]]
            part = jnp.sum(product.reshape(TS // 8, 8, TS), axis=0)
            total = jnp.where(lists[5, k] > 0, total, 0.0) + part
            colseg[k] = total
            return total

        lax.fori_loop(0, count, step, jnp.zeros((8, TS), F32), unroll=8)

        def gather(s, carry):
            wsend[phase, pl.ds(s, 1), :] = jnp.sum(colseg[lists[7, s]], axis=0, keepdims=True)
            return carry

        lax.fori_loop(0, nb, gather, 0, unroll=8)

    for sweep in range(ITERS):
        if sweep:
            row_pass(lambda s: vrecv[0, pl.ds(s, 1), :])
        col_pass(sweep)
        send_all(wsend.at[sweep], wrecv.at[sweep], 2 + 2 * sweep)
        wait_all(wrecv.at[sweep], 2 + 2 * sweep)
        vsend[sweep] = cmass_of / pick(twins, wrecv[sweep])
        send_all(vsend.at[sweep], vrecv.at[sweep], 3 + 2 * sweep)
        if sweep == ITERS - 1:
            cell_v = rowsets[1] / pick(hot_t, wrecv[sweep])
            potential = jnp.log(cell_v) + HALF_LN2 * ysq
            for q in range(tiles):
                cp_out[:, pl.ds(q * TS, TS)] = potential[q : q + 1, :]
        wait_all(vrecv.at[sweep], 3 + 2 * sweep)

    last = vrecv[ITERS - 1]
    for m in range(3):
        vy[m] = last * cells[:, m, :]
    sums = jnp.zeros((TS, TS), F32)
    for m in range(4):
        if m == 3:
            row_pass(lambda s: vrecv[ITERS - 1, pl.ds(s, 1), :])
        else:
            row_pass(lambda s, m=m: vy[m, pl.ds(s, 1), :])

        def place(q, carry, m=m):
            total = jnp.sum(seg[lists[6, q]], axis=1, keepdims=True)
            return jnp.where(iota((TS, TS), 1) == q + m * buckets, total, carry)

        sums = lax.fori_loop(0, buckets, place, sums, unroll=2)
    sums = sums.T
    s0 = sums[3 * buckets : 4 * buckets, :]
    masses = rowsets[0]
    xsq = xs[0] * xs[0] + xs[1] * xs[1] + xs[2] * xs[2]
    potential = jnp.log(masses / s0) + HALF_LN2 * xsq
    for q in range(buckets):
        pp_out[:, pl.ds(q * TS, TS)] = potential[q : q + 1, :]

    spot_row = (lagr_in[...]) // TS
    moves = []
    for m in range(3):
        shift = (sums[m * buckets : (m + 1) * buckets, :] / s0 - xs[m]) * (1.0 / SCALE)
        hi = shift.astype(BF16).astype(F32)
        moves.append((hi, shift - hi))
    placed = jnp.zeros((6 * buckets, TS), F32)
    rows16 = iota((buckets, TS), 0)
    for q in range(buckets):
        on = spot_row[:, q * TS : (q + 1) * TS] == rows16
        stack = [
            jnp.where(on, part[q : q + 1, :], 0.0).astype(BF16) for pair in moves for part in pair
        ]
        placed = placed + jnp.dot(
            jnp.concatenate(stack, axis=0), hot_l[q], preferred_element_type=F32
        )
    for m in range(3):
        base = 2 * m * buckets
        field[m] = placed[base : base + buckets, :] + placed[base + buckets : base + 2 * buckets, :]

    edge = buckets - LB
    sends = [
        (field.at[0, pl.ds(edge, LB)], halo.at[0, pl.ds(0, LB)], (me, right)),
        (field.at[0, pl.ds(0, LB)], halo.at[1, pl.ds(0, LB)], (me, left)),
        (field.at[1], halo.at[2], (up, sl)),
        (field.at[1], halo.at[3], (down, sl)),
    ]
    copies = [
        pltpu.make_async_remote_copy(
            src_ref=src, dst_ref=dst, send_sem=hsem.at[0, i], recv_sem=hsem.at[1, i],
            device_id=device, device_id_type=MESH,
        )
        for i, (src, dst, device) in enumerate(sends)
    ]
    for copy in copies:
        copy.start()
    f2 = field[2]
    lanes = iota((buckets, TS), 1)
    third = jnp.where(lanes == TS - 1, 0.0, pltpu.roll(f2, TS - 1, 1)) - jnp.where(
        lanes == 0, 0.0, pltpu.roll(f2, 1, 1)
    )
    for copy in copies:
        copy.wait()
    f0, f1 = field[0], field[1]
    before = jnp.where(sl > 0, halo[0, 0:LB, :], 0.0)
    after = jnp.where(sl < ns - 1, halo[1, 0:LB, :], 0.0)
    first = jnp.concatenate([f0[LB:], after], axis=0) - jnp.concatenate([before, f0[:edge]], axis=0)
    below = jnp.where(me > 0, halo[2], 0.0)
    above = jnp.where(me < nb - 1, halo[3], 0.0)
    inner = lax.rem(rows16, LB)
    plus = jnp.where(inner == LB - 1, pltpu.roll(above, LB - 1, 0), pltpu.roll(f1, buckets - 1, 0))
    minus = jnp.where(inner == 0, pltpu.roll(below, buckets - (LB - 1), 0), pltpu.roll(f1, 1, 0))
    result = 0.5 * first + 0.5 * (plus - minus)
    result = result + 0.5 * third
    for a in range(buckets // LB):
        div_out[a] = result[a * LB : (a + 1) * LB, :]

    wait_sent(ask, 0)
    wait_sent(pay, 1)
    for sweep in range(ITERS):
        wait_sent(wsend.at[sweep], 2 + 2 * sweep)
        wait_sent(vsend.at[sweep], 3 + 2 * sweep)


def solution(mesh):
    nb, ns = mesh.shape["bricks"], mesh.shape["slab"]

    def on_device(
        part_pos, part_mass, cell_pos, cell_mass, cell_scale,
        req_tile, tile_bucket, tile_slot, tile_count, lagr_index,
    ):
        buckets, tiles = part_pos.shape[2] // TS, cell_pos.shape[2] // TS
        count = tile_bucket.shape[1]
        vmem = pl.BlockSpec(memory_space=pltpu.VMEM)
        smem = pl.BlockSpec(memory_space=pltpu.SMEM)
        return pl.pallas_call(
            functools.partial(kernel, nb, ns, buckets, tiles, count),
            out_shape=(
                jax.ShapeDtypeStruct((1, buckets * TS), F32),
                jax.ShapeDtypeStruct((1, tiles * TS), F32),
                jax.ShapeDtypeStruct((buckets // LB, LB, TS), F32),
            ),
            in_specs=[vmem] * 8 + [smem, vmem],
            out_specs=(vmem, vmem, vmem),
            scratch_shapes=[
                pltpu.VMEM((nb, TS), I32),
                pltpu.VMEM((nb, TS), I32),
                pltpu.VMEM((8, TL), I32),
                pltpu.SMEM((8, TL), I32),
                pltpu.VMEM((3, buckets, TS), F32),
                pltpu.VMEM((3, tiles, TS), F32),
                pltpu.VMEM((3, tiles, TS), F32),
                pltpu.VMEM((3, buckets, TS, TS), F32),
                pltpu.VMEM((buckets, TS, TS), F32),
                pltpu.VMEM((buckets, TS, TS), F32),
                pltpu.VMEM((count, TS, TS), F32),
                pltpu.VMEM((count, TS, TS), F32),
                pltpu.VMEM((count, 8, TS), F32),
                pltpu.VMEM((nb, 4, TS), F32),
                pltpu.VMEM((nb, 4, TS), F32),
                pltpu.VMEM((ITERS, nb, TS), F32),
                pltpu.VMEM((ITERS, nb, TS), F32),
                pltpu.VMEM((ITERS, nb, TS), F32),
                pltpu.VMEM((ITERS, nb, TS), F32),
                pltpu.VMEM((3, nb, TS), F32),
                pltpu.VMEM((buckets, TS, TS), BF16),
                pltpu.VMEM((3, buckets, TS), F32),
                pltpu.VMEM((4, buckets, TS), F32),
                pltpu.SemaphoreType.DMA((2 + 2 * ITERS,)),
                pltpu.SemaphoreType.DMA((2 + 2 * ITERS,)),
                pltpu.SemaphoreType.DMA((2, 4)),
                pltpu.SemaphoreType.DMA,
            ],
            name="sinkhorn",
            compiler_params=pltpu.CompilerParams(
                collective_id=0, has_side_effects=True, vmem_limit_bytes=56 << 20
            ),
        )(
            part_pos, part_mass, cell_pos, cell_mass, cell_scale,
            req_tile, tile_bucket, tile_slot, tile_count, lagr_index,
        )

    device = P(("bricks", "slab"))
    return jax.shard_map(
        on_device,
        mesh=mesh,
        in_specs=(device,) * 10,
        out_specs=(device, device, P("slab", "bricks", None)),
        check_vma=False,
    )
```

time: 642 us -> 79 us (0.12)
  waiting for transfers between devices: 365 us -> 0 us
  blocking collectives: 110 us -> 0 us
  matrix products: 106 us -> 0 us
  Pallas kernels: 0 us -> 72 us
  local copies, waits for them, and re-layouts: 24.4 us -> 5.32 us
  between operations: 14.7 us -> 1.31 us
  starting transfers between devices: 11 us -> 0 us
  other arithmetic: 7.51 us -> 0 us
    reduce_scatter x2 -> x0, waiting for transfers between devices: 264 us -> none  [on_device(): lax.psum_scatter(dense_sums.reshape(brick_count * cell_tiles, tile_width)...]
    all_gather x2 -> x0, blocking collectives: 110 us -> none  [fetch_duals(): return lax.all_gather(values, 'bricks', axis=0, tiled=True)[wanted]]
    dot_general x50 -> x0, matrix products: 106 us -> none  [the longest x27 70 us: row_one_group(): jnp.einsum('tij,tcj->tci', kernel, value_piece, precision=lax.Precision.H...]
    all_gather x2 -> x0, waiting for transfers between devices: 99.7 us -> none  [the longest x1 81.7 us: fetch_duals(): return lax.all_gather(values, 'bricks', axis=0, tiled=True)[wanted]]
    pallas_call x0 -> x1, Pallas kernels: none -> 72 us  [on_device(): pl.pallas_call(functools.partial(kernel, nb, ns, buckets, tiles, count),...]
    ppermute x4 -> x0, starting transfers between devices: 10.8 us -> none  [the longest x2 7.4 us: with_halo(): lax.ppermute(lax.slice_in_dim(block, block.shape[dim] - width, None, axis...]
    gather x12 -> x0, local copies, waits for them, and re-layouts: 9.15 us -> none  [the longest x3 3.44 us: fetch_duals(): return lax.all_gather(values, 'bricks', axis=0, tiled=True)[wanted]]
  transfers between devices with their start and end apart: 8 -> 0, of which waited for: 5 -> 0; matrix products, arithmetic and copies ran while one was open for 1% -> 0% of each run, Pallas kernels for 0% -> 0%
where the time goes in v1:
time: 79 us; the launch traced here: 78.6 us
  Pallas kernels  72 us (91%)
  local copies, waits for them, and re-layouts  5.32 us (7%)
  between operations  1.31 us (2%)
    pallas_call x1, Pallas kernels, on_device(): pl.pallas_call(functools.partial(kernel, nb, ns, buckets, tiles, count),...  72 us
    unnamed x14, local copies, waits for them, and re-layouts  5.32 us

profile of v1, /device:TPU:1, one launch (start us, length us, event | category | flops | bytes accessed | tf_op | source)
XLA Modules:
  0.0 78.6 jit_solution(5736756478848965059)
XLA Ops:
  1.3 0.0 copy-start
  1.3 1.4 %copy.13.pos_in = f32[1,3,2048]{2,1,0:T(4,128)} copy(f32[1,3,2048]{2,0,1:T(1,128)} %param.10) | data formatting | bytes 49152 | tf_op args[0]
  2.7 0.0 copy-done
  2.7 0.0 copy-start.3
  2.7 0.6 copy.14.cpos_in
  3.3 0.0 copy-done.3
  3.3 0.7 copy.15.req_in
  4.0 72.0 %sinkhorn.1 = (f32[1,2048]{1,0:T(1,128)}, f32[1,2048]{1,0:T(1,128)}, f32[4,4,128]{2,1,0:T(4,128)}) custom-call(f32[1,3,2048]{2,1,0:T(4,128)} %copy.13.pos_in, f32[1,2048]{1,0:T(1,128)} %mass_in.1, f32[1,3,2048]{2,1,0:T(4,128)} %copy.14.cpos_in, f32[1,2048]{1,0:T(1,128)} %cmass_in.1, f32[1,2048]{1,0:T(1,128)} %cscale_in.1, s32[64,1]{1,0:T(8,128)} %copy.15.req_in, ...), custom_call_target="tpu_custom_call" | custom-call | tf_op jit(solution)/shard_map/sinkhorn/pallas_call | solution.py:327
  76.0 0.0 copy-start.2
  76.0 1.3 %copy.20 = f32[1,2048]{1,0:T(1,128)} copy(f32[1,2048]{1,0:T(1,128)} %get-tuple-element.6) | data formatting | bytes 16384
  77.3 0.0 copy-done.2
  77.3 0.0 copy-start.1
  77.3 0.6 copy.21
  77.9 0.1 copy-done.1
  78.0 0.6 copy.22
Async XLA Ops:
  1.3 1.4 %copy-start = (f32[1,3,2048]{2,0,1:T(1,128)S(1)}, f32[1,3,2048]{2,0,1:T(1,128)}, u32[]{:S(2)}) copy-start(f32[1,3,2048]{2,0,1:T(1,128)} %param.12) | copy-start | bytes 73732
  2.7 0.7 copy-start.3
  76.0 1.3 %copy-start.2 = (f32[1,2048]{1,0:T(1,128)S(1)}, f32[1,2048]{1,0:T(1,128)}, u32[]{:S(2)}) copy-start(f32[1,2048]{1,0:T(1,128)} %get-tuple-element.7) | copy-start | bytes 24580
  77.3 0.7 copy-start.1

commit v2 on v1

--- a/solution.py
+++ b/solution.py
@@ -43,9 +43,9 @@
 def kernel(
     nb, ns, buckets, tiles, count,
     pos_in, mass_in, cpos_in, cmass_in, cscale_in, req_in, tb_in, ts_in, cnt_in, lagr_in,
-    pp_out, cp_out, div_out,
+    out,
     ask, asked, lists_v, lists, xs, ys, rowsets, xb, mb, ub, kt, seg, colseg,
-    pay, cells, wsend, wrecv, vsend, vrecv, vy, hot_l, field, halo,
+    offer, pay, cells, wsend, wrecv, vsend, vrecv, basis, turned, sums, hot_l, field, halo,
     ssem, rsem, hsem, lsem,
 ):
     me, sl = lax.axis_index("bricks"), lax.axis_index("slab")
@@ -64,9 +64,14 @@
     for other in (left, right):
         pl.semaphore_signal(barrier, inc=1, device_id=(me, other), device_id_type=MESH)
 
+    core, z, y = lax.rem(me, 2), lax.rem(me // 2, 8), me // 16
+
     def send_all(src, dst, phase):
         def one(k, carry):
-            peer = lax.rem(me + k, nb)
+            turn_z, turn_y = k // 8, lax.rem(k // 2, 4)
+            step_z = 4 + (turn_z + 1) // 2 * (1 - 2 * lax.rem(turn_z, 2))
+            step_y = 2 + (turn_y + 1) // 2 * (1 - 2 * lax.rem(turn_y, 2))
+            peer = lax.rem(y + step_y, 4) * 16 + lax.rem(z + step_z, 8) * 2 + lax.rem(core + k + 1, 2)
             pltpu.make_async_remote_copy(
                 src_ref=src.at[peer], dst_ref=dst.at[me],
                 send_sem=ssem.at[phase], recv_sem=rsem.at[phase],
@@ -74,7 +79,7 @@
             ).start()
             return carry
 
-        lax.fori_loop(1, nb, one, 0)
+        lax.fori_loop(0, nb - 1, one, 0)
         pltpu.make_async_copy(src.at[me], dst.at[me], rsem.at[phase]).start()
 
     def wait_all(dst, phase):
@@ -84,10 +89,7 @@
         part = src.at[pl.ds(0, nb - 1)]
         pltpu.make_async_copy(part, part, ssem.at[phase]).wait()
 
-    ask[...] = jnp.broadcast_to(req_in[...], ask.shape)
-
-    pl.semaphore_wait(barrier, nb + 1)
-    send_all(ask, asked, 0)
+    ask[...] = jnp.broadcast_to(req_in[...], (TS, nb)).T
 
     lane = iota((1, TL), 1)
     live = lane < cnt_in[0]
@@ -130,16 +132,19 @@
         part = pl.ds(q * TS, TS)
         rowsets[0, q : q + 1, :] = mass_in[:, part]
         for m in range(3):
-            xs[m, q : q + 1, :] = (pos_in[0, m : m + 1, part] - CENTER[m]) * SCALE
+            xs[m, q : q + 1, :] = (pos_in[m, :, part] - CENTER[m]) * SCALE
     for q in range(tiles):
         part = pl.ds(q * TS, TS)
         rowsets[1, q : q + 1, :] = cmass_in[:, part]
         rowsets[2, q : q + 1, :] = cscale_in[:, part]
         for m in range(3):
-            ys[m, q : q + 1, :] = (cpos_in[0, m : m + 1, part] - CENTER[m]) * SCALE
+            ys[m, q : q + 1, :] = (cpos_in[m, :, part] - CENTER[m]) * SCALE
     ysq = ys[0] * ys[0] + ys[1] * ys[1] + ys[2] * ys[2]
     scaled = rowsets[2] * jnp.exp2(-0.5 * ysq)
-    offer = jnp.concatenate([ys[0], ys[1], ys[2], scaled, rowsets[1]], axis=1)
+    offer[...] = jnp.concatenate(split3(jnp.concatenate([ys[0], ys[1], ys[2], scaled], axis=1)), axis=0)
+
+    pl.semaphore_wait(barrier, nb + 1)
+    send_all(ask, asked, 0)
 
     columns = jnp.concatenate([xs[0], xs[1], xs[2], rowsets[0]], axis=0).T
     for q in range(buckets):
@@ -147,25 +152,26 @@
             xb[m, q] = jnp.broadcast_to(columns[:, m * buckets + q : m * buckets + q + 1], (TS, TS))
         mb[q] = jnp.broadcast_to(columns[:, 3 * buckets + q : 3 * buckets + q + 1], (TS, TS))
 
+    spots = jnp.concatenate(
+        [lagr_in[:, pl.ds(q * TS, TS)] for q in range(buckets)] + [jnp.zeros((TS - buckets, TS), I32)], axis=0
+    )
+    spots_c = (spots & (TS - 1)).T
+    for q in range(buckets):
+        hot_l[pl.ds(q * TS, TS), :] = jnp.where(
+            spots_c[:, q : q + 1] == iota((TS, TS), 1), 1.0, 0.0
+        ).astype(BF16)
+
     wait_all(asked, 0)
     asks = asked[...].astype(F32)
     hot = jnp.where(asks[:, 0:tiles] == iota((nb, tiles), 1).astype(F32), 1.0, 0.0).astype(BF16)
-    chosen = pick(hot, offer)
+    chosen = jnp.dot(jnp.concatenate([hot, hot, hot], axis=1), offer[...], preferred_element_type=F32)
     for m in range(4):
         pay[:, m, :] = chosen[:, m * TS : (m + 1) * TS]
     send_all(pay, cells, 1)
-    cmass_of = chosen[:, 4 * TS :]
+    cmass_of = pick(hot, rowsets[1])
     asks_t = asks.T
     twins = jnp.where(asks[:, 0:nb] == asks_t[0:nb, :], 1.0, 0.0).astype(BF16)
     hot_t = jnp.where(asks_t[0:tiles, :] == iota((tiles, nb), 0).astype(F32), 1.0, 0.0).astype(BF16)
-
-    for q in range(buckets):
-        vy[0, q : q + 1, :] = lagr_in[:, pl.ds(q * TS, TS)].astype(F32)
-    spots = vy[0, 0:buckets, :]
-    spots_c = jnp.concatenate([spots, jnp.zeros((TS - buckets, TS), F32)], axis=0).T
-    for q in range(buckets):
-        spot = jnp.broadcast_to(spots_c[:, q : q + 1], (TS, TS)).astype(I32)
-        hot_l[q] = jnp.where(lax.rem(spot, TS) == iota((TS, TS), 1), 1.0, 0.0).astype(BF16)
 
     to_smem.wait()
     wait_all(cells, 1)
@@ -179,7 +185,7 @@
         seg[k] = total
         return total
 
-    lax.fori_loop(0, count, build, jnp.zeros((TS, TS), F32), unroll=4)
+    lax.fori_loop(0, count, build, jnp.zeros((TS, TS), F32), unroll=8)
 
     def row_pass(value):
         def step(k, total):
@@ -187,14 +193,14 @@
             seg[k] = total
             return total
 
-        lax.fori_loop(0, count, step, jnp.zeros((TS, TS), F32), unroll=4)
+        lax.fori_loop(0, count, step, jnp.zeros((TS, TS), F32), unroll=8)
 
     def col_pass(phase):
         def scale(q, carry):
             ub[q] = mb[q] / jnp.sum(seg[lists[6, q]], axis=1, keepdims=True)
             return carry
 
-        lax.fori_loop(0, buckets, scale, 0, unroll=2)
+        lax.fori_loop(0, buckets, scale, 0, unroll=8)
 
         def step(k, total):
             product = kt[lists[3, k]] * ub[lists[4, k]]
@@ -211,64 +217,86 @@
 
         lax.fori_loop(0, nb, gather, 0, unroll=8)
 
+    def turn(quarter):
+        def step(k, carry):
+            flat = kt[k].T
+            hi = flat.astype(BF16)
+            turned[k, 0:TS, :] = hi
+            turned[k, TS : 2 * TS, :] = (flat - hi.astype(F32)).astype(BF16)
+            return carry
+
+        lax.fori_loop(quarter * count // 4, (quarter + 1) * count // 4, step, 0, unroll=4)
+
     for sweep in range(ITERS):
         if sweep:
             row_pass(lambda s: vrecv[0, pl.ds(s, 1), :])
         col_pass(sweep)
         send_all(wsend.at[sweep], wrecv.at[sweep], 2 + 2 * sweep)
+        turn(2 * sweep)
         wait_all(wrecv.at[sweep], 2 + 2 * sweep)
         vsend[sweep] = cmass_of / pick(twins, wrecv[sweep])
         send_all(vsend.at[sweep], vrecv.at[sweep], 3 + 2 * sweep)
+        turn(2 * sweep + 1)
+        if sweep == 0:
+            for half in range(2):
+                for m in range(3):
+                    basis[:, 4 * half + m, :] = cells[:, m, :]
+                basis[:, 4 * half + 3, :] = jnp.ones((nb, TS), F32)
         if sweep == ITERS - 1:
             cell_v = rowsets[1] / pick(hot_t, wrecv[sweep])
             potential = jnp.log(cell_v) + HALF_LN2 * ysq
-            for q in range(tiles):
-                cp_out[:, pl.ds(q * TS, TS)] = potential[q : q + 1, :]
+            out[1] = potential
         wait_all(vrecv.at[sweep], 3 + 2 * sweep)
 
-    last = vrecv[ITERS - 1]
-    for m in range(3):
-        vy[m] = last * cells[:, m, :]
-    sums = jnp.zeros((TS, TS), F32)
-    for m in range(4):
-        if m == 3:
-            row_pass(lambda s: vrecv[ITERS - 1, pl.ds(s, 1), :])
-        else:
-            row_pass(lambda s, m=m: vy[m, pl.ds(s, 1), :])
-
-        def place(q, carry, m=m):
-            total = jnp.sum(seg[lists[6, q]], axis=1, keepdims=True)
-            return jnp.where(iota((TS, TS), 1) == q + m * buckets, total, carry)
-
-        sums = lax.fori_loop(0, buckets, place, sums, unroll=2)
-    sums = sums.T
-    s0 = sums[3 * buckets : 4 * buckets, :]
-    masses = rowsets[0]
-    xsq = xs[0] * xs[0] + xs[1] * xs[1] + xs[2] * xs[2]
-    potential = jnp.log(masses / s0) + HALF_LN2 * xsq
+    upper = iota((8, TS), 0) < 4
+
+    def last_step(k, total):
+        s = lists[1, k]
+        value = basis[s] * vrecv[ITERS - 1, pl.ds(s, 1), :]
+        hi = value.astype(BF16).astype(F32)
+        left_side = jnp.where(upper, hi, value - hi).astype(BF16)
+        part = jnp.dot(
+            jnp.concatenate([left_side, left_side], axis=1), turned[k], preferred_element_type=F32
+        )
+        total = jnp.where(lists[2, k] > 0, total, 0.0) + part
+        colseg[k] = total
+        return total
+
+    lax.fori_loop(0, count, last_step, jnp.zeros((8, TS), F32), unroll=16)
     for q in range(buckets):
-        pp_out[:, pl.ds(q * TS, TS)] = potential[q : q + 1, :]
-
-    spot_row = (lagr_in[...]) // TS
-    moves = []
-    for m in range(3):
-        shift = (sums[m * buckets : (m + 1) * buckets, :] / s0 - xs[m]) * (1.0 / SCALE)
-        hi = shift.astype(BF16).astype(F32)
-        moves.append((hi, shift - hi))
-    placed = jnp.zeros((6 * buckets, TS), F32)
+        both = colseg[lists[6, q]]
+        both = both[0:4, :] + both[4:8, :]
+        for m in range(4):
+            sums[m, q : q + 1, :] = both[m : m + 1, :]
+    s0 = sums[3]
+
+    spot_row = lagr_in[...] // TS
     rows16 = iota((buckets, TS), 0)
-    for q in range(buckets):
-        on = spot_row[:, q * TS : (q + 1) * TS] == rows16
-        stack = [
-            jnp.where(on, part[q : q + 1, :], 0.0).astype(BF16) for pair in moves for part in pair
+    masks = [spot_row[:, q * TS : (q + 1) * TS] == rows16 for q in range(buckets)]
+
+    def placed(axes):
+        stack = []
+        for m in axes:
+            shift = (sums[m] / s0 - xs[m]) * (1.0 / SCALE)
+            hi = shift.astype(BF16).astype(F32)
+            for part in (hi, shift - hi):
+                stack.append(
+                    jnp.concatenate(
+                        [
+                            jnp.where(masks[q], part[q : q + 1, :], 0.0).astype(BF16)
+                            for q in range(buckets)
+                        ],
+                        axis=1,
+                    )
+                )
+        both = jnp.dot(jnp.concatenate(stack, axis=0), hot_l[...], preferred_element_type=F32)
+        return [
+            both[2 * i * buckets : (2 * i + 1) * buckets, :]
+            + both[(2 * i + 1) * buckets : (2 * i + 2) * buckets, :]
+            for i in range(len(axes))
         ]
-        placed = placed + jnp.dot(
-            jnp.concatenate(stack, axis=0), hot_l[q], preferred_element_type=F32
-        )
-    for m in range(3):
-        base = 2 * m * buckets
-        field[m] = placed[base : base + buckets, :] + placed[base + buckets : base + 2 * buckets, :]
-
+
+    field[0], field[1] = placed((0, 1))
     edge = buckets - LB
     sends = [
         (field.at[0, pl.ds(edge, LB)], halo.at[0, pl.ds(0, LB)], (me, right)),
@@ -285,7 +313,10 @@
     ]
     for copy in copies:
         copy.start()
-    f2 = field[2]
+    xsq = xs[0] * xs[0] + xs[1] * xs[1] + xs[2] * xs[2]
+    potential = jnp.log(rowsets[0] / s0) + HALF_LN2 * xsq
+    out[0] = potential
+    (f2,) = placed((2,))
     lanes = iota((buckets, TS), 1)
     third = jnp.where(lanes == TS - 1, 0.0, pltpu.roll(f2, TS - 1, 1)) - jnp.where(
         lanes == 0, 0.0, pltpu.roll(f2, 1, 1)
@@ -302,9 +333,7 @@
     plus = jnp.where(inner == LB - 1, pltpu.roll(above, LB - 1, 0), pltpu.roll(f1, buckets - 1, 0))
     minus = jnp.where(inner == 0, pltpu.roll(below, buckets - (LB - 1), 0), pltpu.roll(f1, 1, 0))
     result = 0.5 * first + 0.5 * (plus - minus)
-    result = result + 0.5 * third
-    for a in range(buckets // LB):
-        div_out[a] = result[a * LB : (a + 1) * LB, :]
+    out[2] = result + 0.5 * third
 
     wait_sent(ask, 0)
     wait_sent(pay, 1)
@@ -324,15 +353,11 @@
         count = tile_bucket.shape[1]
         vmem = pl.BlockSpec(memory_space=pltpu.VMEM)
         smem = pl.BlockSpec(memory_space=pltpu.SMEM)
-        return pl.pallas_call(
+        out = pl.pallas_call(
             functools.partial(kernel, nb, ns, buckets, tiles, count),
-            out_shape=(
-                jax.ShapeDtypeStruct((1, buckets * TS), F32),
-                jax.ShapeDtypeStruct((1, tiles * TS), F32),
-                jax.ShapeDtypeStruct((buckets // LB, LB, TS), F32),
-            ),
+            out_shape=jax.ShapeDtypeStruct((3, buckets, TS), F32),
             in_specs=[vmem] * 8 + [smem, vmem],
-            out_specs=(vmem, vmem, vmem),
+            out_specs=vmem,
             scratch_shapes=[
                 pltpu.VMEM((nb, TS), I32),
                 pltpu.VMEM((nb, TS), I32),
@@ -347,15 +372,18 @@
                 pltpu.VMEM((count, TS, TS), F32),
                 pltpu.VMEM((count, TS, TS), F32),
                 pltpu.VMEM((count, 8, TS), F32),
+                pltpu.VMEM((3 * tiles, 4 * TS), BF16),
                 pltpu.VMEM((nb, 4, TS), F32),
                 pltpu.VMEM((nb, 4, TS), F32),
                 pltpu.VMEM((ITERS, nb, TS), F32),
                 pltpu.VMEM((ITERS, nb, TS), F32),
                 pltpu.VMEM((ITERS, nb, TS), F32),
                 pltpu.VMEM((ITERS, nb, TS), F32),
-                pltpu.VMEM((3, nb, TS), F32),
-                pltpu.VMEM((buckets, TS, TS), BF16),
-                pltpu.VMEM((3, buckets, TS), F32),
+                pltpu.VMEM((nb, 8, TS), F32),
+                pltpu.VMEM((count, 2 * TS, TS), BF16),
+                pltpu.VMEM((4, buckets, TS), F32),
+                pltpu.VMEM((buckets * TS, TS), BF16),
+                pltpu.VMEM((2, buckets, TS), F32),
                 pltpu.VMEM((4, buckets, TS), F32),
                 pltpu.SemaphoreType.DMA((2 + 2 * ITERS,)),
                 pltpu.SemaphoreType.DMA((2 + 2 * ITERS,)),
@@ -367,9 +395,10 @@
                 collective_id=0, has_side_effects=True, vmem_limit_bytes=56 << 20
             ),
         )(
-            part_pos, part_mass, cell_pos, cell_mass, cell_scale,
-            req_tile, tile_bucket, tile_slot, tile_count, lagr_index,
+            part_pos.transpose(1, 0, 2), part_mass, cell_pos.transpose(1, 0, 2), cell_mass, cell_scale,
+            req_tile.T, tile_bucket, tile_slot, tile_count, lagr_index,
         )
+        return out[0].reshape(1, -1), out[1].reshape(1, -1), out[2].reshape(-1, LB, TS)
 
     device = P(("bricks", "slab"))
     return jax.shard_map(

time: 79 us -> 66.8 us (0.85)
  Pallas kernels: 72 us -> 63.9 us
  local copies, waits for them, and re-layouts: 5.32 us -> 1.34 us
    pallas_call x1, Pallas kernels: 72 us -> 63.9 us  [on_device(): pl.pallas_call(functools.partial(kernel, nb, ns, buckets, tiles, count),...]
    unnamed x14 -> x0, local copies, waits for them, and re-layouts: 5.32 us -> none
    slice x0 -> x1, local copies, waits for them, and re-layouts: none -> 1.34 us  [on_device(): out[2].reshape(-1, LB, TS)]
where the time goes in v2:
time: 66.8 us; the launch traced here: 66.6 us
  Pallas kernels  63.9 us (96%)
  local copies, waits for them, and re-layouts  1.34 us (2%)
  between operations  1.29 us (2%)
    pallas_call x1, Pallas kernels, on_device(): pl.pallas_call(functools.partial(kernel, nb, ns, buckets, tiles, count),...  63.9 us
    slice x1, local copies, waits for them, and re-layouts, on_device(): out[2].reshape(-1, LB, TS)  1.34 us

profile of v2, /device:TPU:1, one launch (start us, length us, event | category | flops | bytes accessed | tf_op | source)
XLA Modules:
  0.0 66.6 jit_solution(13684401665602303527)
XLA Ops:
  1.3 63.9 %sinkhorn.1 = f32[3,16,128]{2,1,0:T(8,128)} custom-call(f32[3,1,2048]{2,1,0:T(1,128)} %bitcast.6, f32[1,2048]{1,0:T(1,128)} %mass_in.1, f32[3,1,2048]{2,1,0:T(1,128)} %bitcast.7, f32[1,2048]{1,0:T(1,128)} %cmass_in.1, f32[1,2048]{1,0:T(1,128)} %cscale_in.1, s32[1,64]{1,0:T(1,128)} %bitcast.11, s32[1,144]{1,0:T(1,128)} %tb_in.1, s32[1,144]{1,0:T(1,128)} %ts_in.1, ...), custom_call_target="tpu_custom_call" | custom-call | tf_op jit(solution)/shard_map/sinkhorn/pallas_call | solution.py:356
  65.2 1.3 %fusion = (f32[1,16,128]{2,1,0:T(8,128)}, f32[1,16,128]{2,1,0:T(8,128)}, f32[1,16,128]{2,1,0:T(8,128)}) fusion(f32[3,16,128]{2,1,0:T(8,128)} %sinkhorn.1), kind=kLoop, calls=%fused_computation | loop fusion | bytes 49152 | tf_op jit(solution)/shard_map/slice | solution.py:401

commit v3 on v2

--- a/solution.py
+++ b/solution.py
@@ -52,26 +52,36 @@
     up, down = lax.rem(me + 1, nb), lax.rem(me + nb - 1, nb)
     right, left = lax.rem(sl + 1, ns), lax.rem(sl + ns - 1, ns)
 
+    core, z, y = lax.rem(me, 2), lax.rem(me // 2, 8), me // 16
+
+    def peer_at(k):
+        turn_z, turn_y = k // 8, lax.rem(k // 2, 4)
+        step_z = 4 + (turn_z + 1) // 2 * (1 - 2 * lax.rem(turn_z, 2))
+        step_y = 2 + (turn_y + 1) // 2 * (1 - 2 * lax.rem(turn_y, 2))
+        return lax.rem(y + step_y, 4) * 16 + lax.rem(z + step_z, 8) * 2 + lax.rem(core + k + 1, 2)
+
+    def place_of(slot):
+        def turn(step):
+            return jnp.where(step < 0, -2 * step - 1, 2 * step)
+
+        off_y = (((slot >> 4) + (4 - y)) & 3) - 2
+        off_z = ((((slot >> 1) & 7) + (8 - z)) & 7) - 4
+        off_core = ((slot & 1) + (2 - core)) & 1
+        return turn(off_z) * 8 + turn(off_y) * 2 + 1 - off_core
+
     barrier = pltpu.get_barrier_semaphore()
 
     def greet(k, carry):
-        pl.semaphore_signal(
-            barrier, inc=1, device_id=(lax.rem(me + k, nb), sl), device_id_type=MESH
-        )
+        pl.semaphore_signal(barrier, inc=1, device_id=(peer_at(k), sl), device_id_type=MESH)
         return carry
 
-    lax.fori_loop(1, nb, greet, 0)
+    lax.fori_loop(0, nb - 1, greet, 0, unroll=7)
     for other in (left, right):
         pl.semaphore_signal(barrier, inc=1, device_id=(me, other), device_id_type=MESH)
 
-    core, z, y = lax.rem(me, 2), lax.rem(me // 2, 8), me // 16
-
     def send_all(src, dst, phase):
         def one(k, carry):
-            turn_z, turn_y = k // 8, lax.rem(k // 2, 4)
-            step_z = 4 + (turn_z + 1) // 2 * (1 - 2 * lax.rem(turn_z, 2))
-            step_y = 2 + (turn_y + 1) // 2 * (1 - 2 * lax.rem(turn_y, 2))
-            peer = lax.rem(y + step_y, 4) * 16 + lax.rem(z + step_z, 8) * 2 + lax.rem(core + k + 1, 2)
+            peer = peer_at(k)
             pltpu.make_async_remote_copy(
                 src_ref=src.at[peer], dst_ref=dst.at[me],
                 send_sem=ssem.at[phase], recv_sem=rsem.at[phase],
@@ -79,7 +89,7 @@
             ).start()
             return carry
 
-        lax.fori_loop(0, nb - 1, one, 0)
+        lax.fori_loop(0, nb - 1, one, 0, unroll=7)
         pltpu.make_async_copy(src.at[me], dst.at[me], rsem.at[phase]).start()
 
     def wait_all(dst, phase):
@@ -96,7 +106,7 @@
     tb = jnp.concatenate([tb_in[...], jnp.zeros((1, TL - count), I32)], axis=1)
     ts = jnp.concatenate([ts_in[...], jnp.zeros((1, TL - count), I32)], axis=1)
     key_b = jnp.where(live, tb, buckets)
-    key_s = jnp.where(live, ts, nb)
+    key_s = jnp.where(live, place_of(ts), nb)
     uni_b, uni_s = key_b * TL + lane, key_s * TL + lane
     zero = jnp.zeros((1, TL), I32)
     cols = jnp.concatenate([uni_b, uni_s, tb, ts, key_b, key_s, zero, zero], axis=0).T
@@ -195,7 +205,7 @@
 
         lax.fori_loop(0, count, step, jnp.zeros((TS, TS), F32), unroll=8)
 
-    def col_pass(phase):
+    def col_pass(sweep):
         def scale(q, carry):
             ub[q] = mb[q] / jnp.sum(seg[lists[6, q]], axis=1, keepdims=True)
             return carry
@@ -209,13 +219,32 @@
             colseg[k] = total
             return total
 
-        lax.fori_loop(0, count, step, jnp.zeros((8, TS), F32), unroll=8)
-
-        def gather(s, carry):
-            wsend[phase, pl.ds(s, 1), :] = jnp.sum(colseg[lists[7, s]], axis=0, keepdims=True)
-            return carry
-
-        lax.fori_loop(0, nb, gather, 0, unroll=8)
+        group = 8
+
+        def steps_and_sends(block, total, sends):
+            first = block * group
+            for i in range(group):
+                total = step(count - nb + first + i, total)
+            for i in range(group):
+                wsend[sweep, pl.ds(first + i, 1), :] = jnp.sum(
+                    colseg[lists[7, first + i]], axis=0, keepdims=True
+                )
+            for i in range(sends):
+                pltpu.make_async_remote_copy(
+                    src_ref=wsend.at[sweep, first + i], dst_ref=wrecv.at[sweep, me],
+                    send_sem=ssem.at[2 + 2 * sweep], recv_sem=rsem.at[2 + 2 * sweep],
+                    device_id=(peer_at(first + i), sl), device_id_type=MESH,
+                ).start()
+            return total
+
+        total = lax.fori_loop(0, count - nb, step, jnp.zeros((8, TS), F32), unroll=8)
+        total = lax.fori_loop(
+            0, nb // group - 1, lambda block, carry: steps_and_sends(block, carry, group), total
+        )
+        steps_and_sends(nb // group - 1, total, group - 1)
+        pltpu.make_async_copy(
+            wsend.at[sweep, nb - 1], wrecv.at[sweep, me], rsem.at[2 + 2 * sweep]
+        ).start()
 
     def turn(quarter):
         def step(k, carry):
@@ -231,7 +260,6 @@
         if sweep:
             row_pass(lambda s: vrecv[0, pl.ds(s, 1), :])
         col_pass(sweep)
-        send_all(wsend.at[sweep], wrecv.at[sweep], 2 + 2 * sweep)
         turn(2 * sweep)
         wait_all(wrecv.at[sweep], 2 + 2 * sweep)
         vsend[sweep] = cmass_of / pick(twins, wrecv[sweep])
@@ -262,7 +290,7 @@
         colseg[k] = total
         return total
 
-    lax.fori_loop(0, count, last_step, jnp.zeros((8, TS), F32), unroll=16)
+    lax.fori_loop(0, count, last_step, jnp.zeros((8, TS), F32), unroll=36)
     for q in range(buckets):
         both = colseg[lists[6, q]]
         both = both[0:4, :] + both[4:8, :]

time: 66.8 us -> 64.8 us (0.970)
  Pallas kernels: 63.9 us -> 62 us
    pallas_call x1, Pallas kernels: 63.9 us -> 62 us  [on_device(): pl.pallas_call(functools.partial(kernel, nb, ns, buckets, tiles, count),...]
where the time goes in v3:
time: 64.8 us; the launch traced here: 64.6 us
  Pallas kernels  62 us (96%)
  local copies, waits for them, and re-layouts  1.34 us (2%)
  between operations  1.29 us (2%)
    pallas_call x1, Pallas kernels, on_device(): pl.pallas_call(functools.partial(kernel, nb, ns, buckets, tiles, count),...  62 us
    slice x1, local copies, waits for them, and re-layouts, on_device(): out[2].reshape(-1, LB, TS)  1.34 us

profile of v3, /device:TPU:1, one launch (start us, length us, event | category | flops | bytes accessed | tf_op | source)
XLA Modules:
  0.0 64.6 jit_solution(10392534266280153187)
XLA Ops:
  1.3 62.0 %sinkhorn.1 = f32[3,16,128]{2,1,0:T(8,128)} custom-call(f32[3,1,2048]{2,1,0:T(1,128)} %bitcast.6, f32[1,2048]{1,0:T(1,128)} %mass_in.1, f32[3,1,2048]{2,1,0:T(1,128)} %bitcast.7, f32[1,2048]{1,0:T(1,128)} %cmass_in.1, f32[1,2048]{1,0:T(1,128)} %cscale_in.1, s32[1,64]{1,0:T(1,128)} %bitcast.11, s32[1,144]{1,0:T(1,128)} %tb_in.1, s32[1,144]{1,0:T(1,128)} %ts_in.1, ...), custom_call_target="tpu_custom_call" | custom-call | tf_op jit(solution)/shard_map/sinkhorn/pallas_call | solution.py:384
  63.2 1.3 %fusion = (f32[1,16,128]{2,1,0:T(8,128)}, f32[1,16,128]{2,1,0:T(8,128)}, f32[1,16,128]{2,1,0:T(8,128)}) fusion(f32[3,16,128]{2,1,0:T(8,128)} %sinkhorn.1), kind=kLoop, calls=%fused_computation | loop fusion | bytes 49152 | tf_op jit(solution)/shard_map/slice | solution.py:429

commit v4 on v3

--- a/solution.py
+++ b/solution.py
@@ -42,8 +42,9 @@
 
 def kernel(
     nb, ns, buckets, tiles, count,
-    pos_in, mass_in, cpos_in, cmass_in, cscale_in, req_in, tb_in, ts_in, cnt_in, lagr_in,
+    pos_far, mass_far, cpos_far, cmass_far, cscale_far, req_far, tb_far, ts_far, cnt_in, lagr_far,
     out,
+    pos_in, mass_in, cpos_in, cmass_in, cscale_in, req_in, tb_in, ts_in, lagr_in, isem,
     ask, asked, lists_v, lists, xs, ys, rowsets, xb, mb, ub, kt, seg, colseg,
     offer, pay, cells, wsend, wrecv, vsend, vrecv, basis, turned, sums, hot_l, field, halo,
     ssem, rsem, hsem, lsem,
@@ -78,6 +79,19 @@
     lax.fori_loop(0, nb - 1, greet, 0, unroll=7)
     for other in (left, right):
         pl.semaphore_signal(barrier, inc=1, device_id=(me, other), device_id_type=MESH)
+
+    loads = [
+        pltpu.make_async_copy(far, near, isem.at[i])
+        for i, (far, near) in enumerate(
+            (
+                (req_far, req_in), (tb_far, tb_in), (ts_far, ts_in), (pos_far, pos_in),
+                (mass_far, mass_in), (cpos_far, cpos_in), (cmass_far, cmass_in),
+                (cscale_far, cscale_in), (lagr_far, lagr_in),
+            )
+        )
+    ]
+    for load in loads:
+        load.start()
 
     def send_all(src, dst, phase):
         def one(k, carry):
@@ -99,6 +113,8 @@
         part = src.at[pl.ds(0, nb - 1)]
         pltpu.make_async_copy(part, part, ssem.at[phase]).wait()
 
+    for load in loads:
+        load.wait()
     ask[...] = jnp.broadcast_to(req_in[...], (TS, nb)).T
 
     lane = iota((1, TL), 1)
@@ -254,7 +270,7 @@
             turned[k, TS : 2 * TS, :] = (flat - hi.astype(F32)).astype(BF16)
             return carry
 
-        lax.fori_loop(quarter * count // 4, (quarter + 1) * count // 4, step, 0, unroll=4)
+        lax.fori_loop(quarter * count // 4, (quarter + 1) * count // 4, step, 0, unroll=2)
 
     for sweep in range(ITERS):
         if sweep:
@@ -381,12 +397,23 @@
         count = tile_bucket.shape[1]
         vmem = pl.BlockSpec(memory_space=pltpu.VMEM)
         smem = pl.BlockSpec(memory_space=pltpu.SMEM)
+        away = pl.BlockSpec(memory_space=pl.ANY)
         out = pl.pallas_call(
             functools.partial(kernel, nb, ns, buckets, tiles, count),
             out_shape=jax.ShapeDtypeStruct((3, buckets, TS), F32),
-            in_specs=[vmem] * 8 + [smem, vmem],
+            in_specs=[away] * 8 + [smem, away],
             out_specs=vmem,
             scratch_shapes=[
+                pltpu.VMEM((3, 1, buckets * TS), F32),
+                pltpu.VMEM((1, buckets * TS), F32),
+                pltpu.VMEM((3, 1, tiles * TS), F32),
+                pltpu.VMEM((1, tiles * TS), F32),
+                pltpu.VMEM((1, tiles * TS), F32),
+                pltpu.VMEM((1, nb), I32),
+                pltpu.VMEM((1, count), I32),
+                pltpu.VMEM((1, count), I32),
+                pltpu.VMEM((1, buckets * TS), I32),
+                pltpu.SemaphoreType.DMA((9,)),
                 pltpu.VMEM((nb, TS), I32),
                 pltpu.VMEM((nb, TS), I32),
                 pltpu.VMEM((8, TL), I32),

time: 64.8 us -> 64.4 us (level)
  no operation moved by 1% of the time
where the time goes in v4:
time: 64.4 us; the launch traced here: 64.2 us
  Pallas kernels  61.6 us (96%)
  local copies, waits for them, and re-layouts  1.34 us (2%)
  between operations  1.29 us (2%)
    pallas_call x1, Pallas kernels, on_device(): pl.pallas_call(functools.partial(kernel, nb, ns, buckets, tiles, count),...  61.6 us
    slice x1, local copies, waits for them, and re-layouts, on_device(): out[2].reshape(-1, LB, TS)  1.34 us

profile of v4, /device:TPU:1, one launch (start us, length us, event | category | flops | bytes accessed | tf_op | source)
XLA Modules:
  0.0 64.2 jit_solution(718645890058264132)
XLA Ops:
  1.3 61.6 %sinkhorn.1 = f32[3,16,128]{2,1,0:T(8,128)} custom-call(f32[3,1,2048]{2,1,0:T(1,128)} %bitcast.6, f32[1,2048]{1,0:T(1,128)} %mass_far.1, f32[3,1,2048]{2,1,0:T(1,128)} %bitcast.7, f32[1,2048]{1,0:T(1,128)} %cmass_far.1, f32[1,2048]{1,0:T(1,128)} %cscale_far.1, s32[1,64]{1,0:T(1,128)} %bitcast.11, s32[1,144]{1,0:T(1,128)} %tb_far.1, s32[1,144]{1,0:T(1,128)} %ts_far.1, ...), custom_call_target="tpu_custom_call" | custom-call | tf_op jit(solution)/shard_map/sinkhorn/pallas_call | solution.py:401
  62.9 1.3 %fusion = (f32[1,16,128]{2,1,0:T(8,128)}, f32[1,16,128]{2,1,0:T(8,128)}, f32[1,16,128]{2,1,0:T(8,128)}) fusion(f32[3,16,128]{2,1,0:T(8,128)} %sinkhorn.1), kind=kLoop, calls=%fused_computation | loop fusion | bytes 49152 | tf_op jit(solution)/shard_map/slice | solution.py:456

commit v5 on v4

--- a/solution.py
+++ b/solution.py
@@ -235,7 +235,7 @@
             colseg[k] = total
             return total
 
-        group = 8
+        group = 16
 
         def steps_and_sends(block, total, sends):
             first = block * group

time: 64.4 us -> 64.4 us (level)
  no operation moved by 1% of the time
where the time goes in v5:
time: 64.4 us; the launch traced here: 64.2 us
  Pallas kernels  61.5 us (95%)
  local copies, waits for them, and re-layouts  1.34 us (2%)
  between operations  1.29 us (2%)
    pallas_call x1, Pallas kernels, on_device(): pl.pallas_call(functools.partial(kernel, nb, ns, buckets, tiles, count),...  61.5 us
    slice x1, local copies, waits for them, and re-layouts, on_device(): out[2].reshape(-1, LB, TS)  1.34 us

profile of v5, /device:TPU:1, one launch (start us, length us, event | category | flops | bytes accessed | tf_op | source)
XLA Modules:
  0.0 64.2 jit_solution(6372665129804108660)
XLA Ops:
  1.3 61.5 %sinkhorn.1 = f32[3,16,128]{2,1,0:T(8,128)} custom-call(f32[3,1,2048]{2,1,0:T(1,128)} %bitcast.6, f32[1,2048]{1,0:T(1,128)} %mass_far.1, f32[3,1,2048]{2,1,0:T(1,128)} %bitcast.7, f32[1,2048]{1,0:T(1,128)} %cmass_far.1, f32[1,2048]{1,0:T(1,128)} %cscale_far.1, s32[1,64]{1,0:T(1,128)} %bitcast.11, s32[1,144]{1,0:T(1,128)} %tb_far.1, s32[1,144]{1,0:T(1,128)} %ts_far.1, ...), custom_call_target="tpu_custom_call" | custom-call | tf_op jit(solution)/shard_map/sinkhorn/pallas_call | solution.py:401
  62.8 1.3 %fusion = (f32[1,16,128]{2,1,0:T(8,128)}, f32[1,16,128]{2,1,0:T(8,128)}, f32[1,16,128]{2,1,0:T(8,128)}) fusion(f32[3,16,128]{2,1,0:T(8,128)} %sinkhorn.1), kind=kLoop, calls=%fused_computation | loop fusion | bytes 49152 | tf_op jit(solution)/shard_map/slice | solution.py:456
